TPU v7x, 256 devices: a whole 4x4x8 slice. The times are simulated.
256 devices in a mesh: lsec: 16 (over x, z_lo), rsec: 16 (over z_hi, y, core).
Axes of the slice: x: 4, y: 4, z: 8 (z_hi: 2, z_lo: 4; z = z_hi * 4 + z_lo), core: 2. Of those that a mesh axis runs over, the one named last changes fastest.
Arguments:
- states: float32 [2, 10240, 10240], P(None, 'lsec', 'rsec'), may hold values from -6 to 6
- left_env: float32 [16, 640, 640], P('lsec', 'rsec'), may hold values from -0.25 to 0.25
- right_env: float32 [16, 640, 640], P('rsec', 'lsec'), may hold values from -0.25 to 0.25
- left_op: float32 [16, 640, 640], P('lsec', 'rsec'), may hold values from -0.25 to 0.25
- right_op: float32 [16, 640, 640], P('rsec', 'lsec'), may hold values from -0.25 to 0.25
- sizes_left: int32 [16], P('lsec'), may hold values from 320 to 640
- sizes_right: int32 [16], P('rsec'), may hold values from 320 to 640
Outputs:
- applied: float32 [2, 10240, 10240], P(None, 'lsec', 'rsec')
All inputs are finite; a program needn't handle non-finite values.
Results may differ from a plain program's by a relative error of at most 0.000059.
Values sent between devices are 32-bit elements; how exact they have to be, the bound alone decides.
A program may use at most 128 MiB of HBM per device.

v0:
```python
import jax
import jax.numpy as jnp
from jax import lax
from jax.sharding import PartitionSpec as P

HI = lax.Precision.HIGHEST


def in_order(pieces, dim):
    pieces = jnp.moveaxis(pieces, 0, dim)
    dims = pieces.shape
    return pieces.reshape(*dims[:dim], dims[dim] * dims[dim + 1], *dims[dim + 2 :])


def from_everyone(array, axis):
    size = lax.axis_size(axis)
    return lax.all_to_all(
        jnp.broadcast_to(array[None], (size, *array.shape)), axis, 0, 0, tiled=True
    )


def gathered_copies(array, axis, dim):
    return in_order(from_everyone(array, axis), dim)


def passed_along(value, axis, steps):
    count = lax.axis_size(axis)
    leading, last = (max(0, -steps), min(count, count - steps))
    return lax.ppermute(value, axis, [(source, source + steps) for source in range(leading, last)])


def on_device(states, left_env, right_env, left_op, right_op, sizes_left, sizes_right):
    width = states.shape[1]
    rows = jnp.arange(width, dtype=jnp.int32)
    mask = (rows[:, None] < sizes_left[0]).astype(jnp.float32) * (
        rows[None, :] < sizes_right[0]
    ).astype(jnp.float32)
    masked = states * mask[None]
    local = jnp.einsum(
        "ab,rbc->rac", lax.all_gather(left_env, "rsec", axis=1, tiled=True)[0], masked, precision=HI
    )
    local = local + jnp.einsum(
        "rbc,dc->rbd", masked, gathered_copies(right_env, "lsec", 1)[0], precision=HI
    )
    full_op_l = lax.all_gather(left_op, "rsec", axis=1, tiled=True)
    full_op_r = gathered_copies(right_op, "lsec", 1)
    oper_l = full_op_l[0]
    oper_r = full_op_r[0]
    lowered = passed_along(masked, "lsec", 1)
    moved = passed_along(lowered, "rsec", -1)
    inner = jnp.einsum("rbc,dc->rbd", moved, oper_r, precision=HI)
    hop = jnp.einsum("ab,rbd->rad", oper_l, inner, precision=HI)
    right_part = jnp.einsum("rbc,cd->rbd", masked, oper_r, precision=HI)
    source = jnp.einsum("ba,rbd->rad", oper_l, right_part, precision=HI)
    halfway = passed_along(source, "lsec", -1)
    back = passed_along(halfway, "rsec", 1)
    return (local + hop + back) * mask[None]


def solution(mesh):
    in_specs = (
        P(None, "lsec", "rsec"),
        P("lsec", "rsec", None),
        P("rsec", "lsec", None),
        P("lsec", "rsec", None),
        P("rsec", "lsec", None),
        P("lsec"),
        P("rsec"),
    )
    out_specs = P(None, "lsec", "rsec")
    return jax.shard_map(
        on_device, mesh=mesh, in_specs=in_specs, out_specs=out_specs, check_vma=False
    )
```

profile of v0, /device:TPU:198, one launch (start us, length us, event | category | flops | bytes accessed | tf_op | source)
XLA Modules:
  0.0 385.5 jit_solution(120232525778104379)
XLA Ops:
  6.5 0.0 copy-start.4
  6.5 2.3 broadcast_in_dim.11
  8.9 7.0 %all-to-all-start.1 = ((f32[16,1,40,640]{3,2,1,0:T(8,128)}), f32[16,1,40,640]{3,2,1,0:T(8,128)}, u32[]{:S(2)}, u32[]{:S(2)}) async-start(f32[16,1,40,640]{3,2,1,0:T(8,128)} %broadcast_in_dim.11), calls=%async_computation.1 | async-start | bytes 3276800 | tf_op jit(solution)/shard_map/all_to_all | solution.py:17
  15.9 0.0 all-gather.5.cloned.1.call-start
  16.0 0.7 all-gather.5.cloned.1.call-update
  17.9 0.0 copy-done.4
  17.9 3.0 copy.12
  20.9 0.2 broadcast_multiply_fusion.1
  21.1 0.0 copy-start
  21.1 2.8 broadcast_multiply_fusion
  23.9 0.0 copy-done
  23.9 3.4 collective-permute-start
  27.3 25.9 %all-to-all-done.1 = f32[16,1,40,640]{3,2,1,0:T(8,128)} async-done(((f32[16,1,40,640]{3,2,1,0:T(8,128)}), f32[16,1,40,640]{3,2,1,0:T(8,128)}, u32[]{:S(2)}, u32[]{:S(2)}) %all-to-all-start.1) | async-done | bytes 1638432 | tf_op jit(solution)/shard_map/all_to_all | solution.py:17
  53.2 11.1 %fusion.11 = f32[2,640,640]{1,2,0:T(8,128)} fusion(f32[2,640,640]{1,2,0:T(8,128)S(1)} %broadcast_multiply_fusion, f32[640,640,1]{1,0,2:T(8,128)} %bitcast.10), kind=kOutput, calls=%fused_computation.18 | convolution fusion | flops 6291456000 | bytes 8192000 | tf_op jit(solution)/shard_map/rbc,cd->rbd/dot_general | solution.py:53
  64.4 0.0 copy-start.5
  64.4 20.5 %all-gather.5.cloned.1.call-done = f32[1,640,640]{2,1,0:T(8,128)} async-done(((f32[1,40,640]{2,1,0:T(8,128)}), f32[1,640,640]{2,1,0:T(8,128)}) %all-gather.5.cloned.1.call-update) | async-done | bytes 1638416 | tf_op jit(solution)/shard_map/all_gather | solution.py:45
  84.9 12.8 %convolution_bitcast_fusion = f32[2,640,640]{1,2,0:T(8,128)} fusion(f32[2,640,640]{1,2,0:T(8,128)} %fusion.11, f32[1,640,640]{2,1,0:T(8,128)} %all-gather.5.cloned.1.call-done), kind=kOutput, calls=%fused_computation.4 | convolution fusion | flops 6291456000 | bytes 8192000 | tf_op jit(solution)/shard_map/ba,rbd->rad/dot_general | solution.py:54
  97.7 59.5 %collective-permute-start.2 = (f32[2,640,640]{1,2,0:T(8,128)}, f32[2,640,640]{1,2,0:T(8,128)}, u32[]{:S(2)}, u32[]{:S(2)}) collective-permute-start(f32[2,640,640]{1,2,0:T(8,128)} %convolution_bitcast_fusion), channel_id=1, source_target_pairs={{16,0},{32,16},{48,32},{64,48},{80,64},{96,80},{112,96},{128,112},... | collective-permute-start | bytes 9830408 | tf_op jit(solution)/shard_map/ppermute | solution.py:29
  157.2 0.0 copy-done.5
  157.2 1.3 broadcast_in_dim.9
  158.5 10.0 %all-to-all-start = ((f32[16,1,40,640]{3,2,1,0:T(8,128)}), f32[16,1,40,640]{3,2,1,0:T(8,128)}, u32[]{:S(2)}, u32[]{:S(2)}) async-start(f32[16,1,40,640]{3,2,1,0:T(8,128)} %broadcast_in_dim.9), calls=%async_computation | async-start | bytes 3276800 | tf_op jit(solution)/shard_map/all_to_all | solution.py:17
  168.5 0.0 all-gather.3.cloned.1.call-start
  168.5 0.7 all-gather.3.cloned.1.call-update
  169.2 0.0 collective-permute-done
  169.2 3.6 collective-permute-start.1
  172.9 119.7 %collective-permute-done.2 = f32[2,640,640]{1,2,0:T(8,128)} collective-permute-done((f32[2,640,640]{1,2,0:T(8,128)}, f32[2,640,640]{1,2,0:T(8,128)}, u32[]{:S(2)}, u32[]{:S(2)}) %collective-permute-start.2) | collective-permute-done | bytes 3276832 | tf_op jit(solution)/shard_map/ppermute | solution.py:29
  292.5 1.9 collective-permute-start.3
  294.4 15.3 %all-to-all-done = f32[16,1,40,640]{3,2,1,0:T(8,128)} async-done(((f32[16,1,40,640]{3,2,1,0:T(8,128)}), f32[16,1,40,640]{3,2,1,0:T(8,128)}, u32[]{:S(2)}, u32[]{:S(2)}) %all-to-all-start) | async-done | bytes 1638432 | tf_op jit(solution)/shard_map/all_to_all | solution.py:17
  309.8 10.8 %fusion.9 = f32[2,640,640]{1,2,0:T(8,128)} fusion(f32[2,640,640]{1,2,0:T(8,128)S(1)} %broadcast_multiply_fusion, f32[640,640,1]{1,0,2:T(8,128)} %bitcast.7), kind=kOutput, calls=%fused_computation.16 | convolution fusion | flops 6291456000 | bytes 8192000 | tf_op jit(solution)/shard_map/rbc,dc->rbd/dot_general | solution.py:42
  320.6 0.0 all-gather.3.cloned.1.call-done
  320.6 11.0 %fusion.5 = f32[2,640,640]{2,1,0:T(8,128)S(1)} fusion(f32[2,640,640]{1,2,0:T(8,128)S(1)} %broadcast_multiply_fusion, f32[1,640,640]{2,1,0:T(8,128)} %all-gather.3.cloned.1.call-done), kind=kOutput, calls=%fused_computation.8 | convolution fusion | flops 6291456000 | bytes 8192000 | tf_op jit(solution)/shard_map/ab,rbc->rac/dot_general | solution.py:39
  331.6 0.0 copy-start.3
  331.6 7.1 %collective-permute-done.1 = f32[2,640,640]{1,2,0:T(8,128)} collective-permute-done((f32[2,640,640]{1,2,0:T(8,128)}, f32[2,640,640]{1,2,0:T(8,128)}, u32[]{:S(2)}, u32[]{:S(2)}) %collective-permute-start.1) | collective-permute-done | bytes 3276832 | tf_op jit(solution)/shard_map/ppermute | solution.py:29
  338.7 11.4 %fusion.10 = f32[2,640,640]{1,2,0:T(8,128)S(1)} fusion(f32[2,640,640]{1,2,0:T(8,128)} %collective-permute-done.1, f32[640,640,1]{1,0,2:T(8,128)} %bitcast.10), kind=kOutput, calls=%fused_computation.17 | convolution fusion | flops 6291456000 | bytes 8192000 | tf_op jit(solution)/shard_map/rbc,dc->rbd/dot_general | solution.py:51
  350.1 0.0 copy-done.3
  350.1 0.0 copy-start.1
  350.1 0.0 copy-start.2
  350.1 9.8 %fusion.3 = f32[2,640,640]{2,1,0:T(8,128)S(1)} fusion(f32[2,640,640]{1,2,0:T(8,128)S(1)} %fusion.10, f32[1,640,640]{2,1,0:T(8,128)S(1)} %copy-done.3), kind=kOutput, calls=%fused_computation.6 | convolution fusion | flops 6291456000 | bytes 8192000 | tf_op jit(solution)/shard_map/ab,rbd->rad/dot_general | solution.py:52
  360.0 12.6 %collective-permute-done.3 = f32[2,640,640]{1,2,0:T(8,128)} collective-permute-done((f32[2,640,640]{1,2,0:T(8,128)}, f32[2,640,640]{1,2,0:T(8,128)}, u32[]{:S(2)}, u32[]{:S(2)}) %collective-permute-start.3) | collective-permute-done | bytes 3276832 | tf_op jit(solution)/shard_map/ppermute | solution.py:29
  372.5 0.0 copy-done.1
  372.5 0.0 copy-done.2
  372.5 2.8 fusion.1
  375.3 3.0 copy.15
  (1 shorter events, 0.0 us)
Async XLA Ops:
  6.5 11.4 %copy-start.4 = (f32[2,640,640]{2,1,0:T(8,128)S(1)}, f32[2,640,640]{2,1,0:T(8,128)}, u32[]{:S(2)}) copy-start(f32[2,640,640]{2,1,0:T(8,128)} %param.7) | copy-start | bytes 9830404
  8.9 44.4 %all-to-all-start.1 = ((f32[16,1,40,640]{3,2,1,0:T(8,128)}), f32[16,1,40,640]{3,2,1,0:T(8,128)}, u32[]{:S(2)}, u32[]{:S(2)}) async-start(f32[16,1,40,640]{3,2,1,0:T(8,128)} %broadcast_in_dim.11), calls=%async_computation.1 | async-start | bytes 3276800 | tf_op jit(solution)/shard_map/all_to_all | solution.py:17
  15.9 68.9 %all-gather.5.cloned.1.call-start = ((), (), s32[]{:S(2)}) async-start(), calls=%async_computation.3 | async-start | bytes 1740800 | tf_op jit(solution)/shard_map/all_gather | solution.py:45
  21.1 2.8 copy-start
  23.9 145.3 %collective-permute-start = (f32[2,640,640]{1,2,0:T(8,128)S(1)}, f32[2,640,640]{1,2,0:T(8,128)}, u32[]{:S(2)}, u32[]{:S(2)}) collective-permute-start(f32[2,640,640]{1,2,0:T(8,128)S(1)} %broadcast_multiply_fusion), channel_id=1, source_target_pairs={{0,16},{16,32},{32,48},{48,64},{64,80},{80,96},{96,112},{112,128},... | collective-permute-start | bytes 9830408 | tf_op jit(solution)/shard_map/ppermute | solution.py:29
  64.4 92.9 %copy-start.5 = (f32[1,40,640]{2,1,0:T(8,128)S(1)}, f32[1,40,640]{2,1,0:T(8,128)}, u32[]{:S(2)}) copy-start(f32[1,40,640]{2,1,0:T(8,128)} %param.9) | copy-start | bytes 307204
  97.7 194.8 %collective-permute-start.2 = (f32[2,640,640]{1,2,0:T(8,128)}, f32[2,640,640]{1,2,0:T(8,128)}, u32[]{:S(2)}, u32[]{:S(2)}) collective-permute-start(f32[2,640,640]{1,2,0:T(8,128)} %convolution_bitcast_fusion), channel_id=1, source_target_pairs={{16,0},{32,16},{48,32},{64,48},{80,64},{96,80},{112,96},{128,112},... | collective-permute-start | bytes 9830408 | tf_op jit(solution)/shard_map/ppermute | solution.py:29
  158.5 151.3 %all-to-all-start = ((f32[16,1,40,640]{3,2,1,0:T(8,128)}), f32[16,1,40,640]{3,2,1,0:T(8,128)}, u32[]{:S(2)}, u32[]{:S(2)}) async-start(f32[16,1,40,640]{3,2,1,0:T(8,128)} %broadcast_in_dim.9), calls=%async_computation | async-start | bytes 3276800 | tf_op jit(solution)/shard_map/all_to_all | solution.py:17
  168.5 152.2 %all-gather.3.cloned.1.call-start = ((), (), s32[]{:S(2)}) async-start(), calls=%async_computation.2 | async-start | bytes 1740800 | tf_op jit(solution)/shard_map/all_gather | solution.py:40
  169.2 169.5 %collective-permute-start.1 = (f32[2,640,640]{1,2,0:T(8,128)}, f32[2,640,640]{1,2,0:T(8,128)}, u32[]{:S(2)}, u32[]{:S(2)}) collective-permute-start(f32[2,640,640]{1,2,0:T(8,128)} %collective-permute-done), channel_id=1, source_target_pairs={{1,0},{2,1},{3,2},{4,3},{5,4},{6,5},{7,6},{8,7},{9,8},{10,9},{11,1... | collective-permute-start | bytes 9830408 | tf_op jit(solution)/shard_map/ppermute | solution.py:29
  292.5 80.0 %collective-permute-start.3 = (f32[2,640,640]{1,2,0:T(8,128)}, f32[2,640,640]{1,2,0:T(8,128)}, u32[]{:S(2)}, u32[]{:S(2)}) collective-permute-start(f32[2,640,640]{1,2,0:T(8,128)} %collective-permute-done.2), channel_id=1, source_target_pairs={{0,1},{1,2},{2,3},{3,4},{4,5},{5,6},{6,7},{7,8},{8,9},{9,10},{10,1... | collective-permute-start | bytes 9830408 | tf_op jit(solution)/shard_map/ppermute | solution.py:29
  331.6 18.4 %copy-start.3 = (f32[1,640,640]{2,1,0:T(8,128)S(1)}, f32[1,640,640]{2,1,0:T(8,128)}, u32[]{:S(2)}) copy-start(f32[1,640,640]{2,1,0:T(8,128)} %all-gather.5.cloned.1.call-done) | copy-start | bytes 4915204
  350.1 22.4 %copy-start.1 = (f32[640,640]{0,1:T(8,128)S(1)}, f32[640,640]{0,1:T(8,128)}, u32[]{:S(2)}) copy-start(f32[640,640]{0,1:T(8,128)} %copy-done) | copy-start | bytes 4915204
  350.1 22.4 %copy-start.2 = (f32[2,640,640]{1,2,0:T(8,128)S(1)}, f32[2,640,640]{1,2,0:T(8,128)}, u32[]{:S(2)}) copy-start(f32[2,640,640]{1,2,0:T(8,128)} %fusion.9) | copy-start | bytes 9830404
Sparse Core Ops, SparseCore 0:
  19.4 65.4 all-gather.4
  171.9 105.4 all-gather.2
where the time goes:
time: 393 us; the launch traced here: 386 us
  waiting for transfers between devices  202 us (51%)
  starting transfers between devices  85.5 us (22%)
  matrix products  66.9 us (17%)
  between operations  15.3 us (4%)
  local copies, waits for them, and re-layouts  9.54 us (2%)
  other arithmetic  5.75 us (1%)
    ppermute x4, waiting for transfers between devices, passed_along(): lax.ppermute(value, axis, [(source, source + steps) for source in range(l...  139 us
    ppermute x4, starting transfers between devices, passed_along(): lax.ppermute(value, axis, [(source, source + steps) for source in range(l...  68.4 us
    all_to_all x2, waiting for transfers between devices, from_everyone(): lax.all_to_all(jnp.broadcast_to(array[None], (size, *array.shape)), axis,...  41.3 us
    all_gather x1, waiting for transfers between devices, on_device(): full_op_l = lax.all_gather(left_op, 'rsec', axis=1, tiled=True)  20.5 us
    all_to_all x2, starting transfers between devices, from_everyone(): lax.all_to_all(jnp.broadcast_to(array[None], (size, *array.shape)), axis,...  17 us
    dot_general x1, matrix products, on_device(): source = jnp.einsum('ba,rbd->rad', oper_l, right_part, precision=HI)  12.8 us
    dot_general x1, matrix products, on_device(): inner = jnp.einsum('rbc,dc->rbd', moved, oper_r, precision=HI)  11.4 us
    dot_general x1, matrix products, on_device(): right_part = jnp.einsum('rbc,cd->rbd', masked, oper_r, precision=HI)  11.1 us
  transfers between devices with their start and end apart: 8, of which 6 were waited for; matrix products, arithmetic and copies ran while one was open for 19% of the time, Pallas kernels for 0%

commit v1 on v0

v1 whole, which is shorter than its diff:
```python
import jax
import jax.numpy as jnp
from jax import lax
from jax.sharding import PartitionSpec as P

HI = lax.Precision.HIGH


def shifted(value, step):
    n, m = lax.axis_size("lsec"), lax.axis_size("rsec")
    pairs = [
        (i * m + j, (i + step) * m + j - step)
        for i in range(n)
        for j in range(m)
        if 0 <= i + step < n and 0 <= j - step < m
    ]
    return lax.ppermute(value, ("lsec", "rsec"), pairs)


def on_device(states, left_env, right_env, left_op, right_op, sizes_left, sizes_right):
    width = states.shape[1]
    rows = jnp.arange(width, dtype=jnp.int32)
    mask = (rows[:, None] < sizes_left[0]).astype(jnp.float32) * (
        rows[None, :] < sizes_right[0]
    ).astype(jnp.float32)
    masked = states * mask[None]
    moved = shifted(masked, 1)
    left = lax.all_gather(jnp.concatenate([left_env, left_op]), "rsec", axis=1, tiled=True)
    right = lax.all_gather(jnp.concatenate([right_env, right_op]), "lsec", axis=1, tiled=True)
    env_l, oper_l, env_r, oper_r = left[0], left[1], right[0], right[1]
    right_part = jnp.einsum("rbc,cd->rbd", masked, oper_r, precision=HI)
    source = jnp.einsum("ba,rbd->rad", oper_l, right_part, precision=HI)
    back = shifted(source, -1)
    local = jnp.einsum("ab,rbc->rac", env_l, masked, precision=HI)
    local = local + jnp.einsum("rbc,dc->rbd", masked, env_r, precision=HI)
    inner = jnp.einsum("rbc,dc->rbd", moved, oper_r, precision=HI)
    hop = jnp.einsum("ab,rbd->rad", oper_l, inner, precision=HI)
    return (local + hop + back) * mask[None]


def solution(mesh):
    in_specs = (
        P(None, "lsec", "rsec"),
        P("lsec", "rsec", None),
        P("rsec", "lsec", None),
        P("lsec", "rsec", None),
        P("rsec", "lsec", None),
        P("lsec"),
        P("rsec"),
    )
    out_specs = P(None, "lsec", "rsec")
    return jax.shard_map(
        on_device, mesh=mesh, in_specs=in_specs, out_specs=out_specs, check_vma=False
    )
```

time: 393 us -> 411 us (1.046); the launches traced: 386 us -> 411 us
  waiting for transfers between devices: 202 us -> 339 us
  starting transfers between devices: 85.5 us -> 7.2 us
  matrix products: 66.9 us -> 35.9 us
    all_gather x2, waiting for transfers between devices: 20.5 us -> 233 us  [the longest x1 150 us: on_device(): lax.all_gather(jnp.concatenate([right_env, right_op]), 'lsec', axis=1, ti...]
    ppermute x4 -> x2, starting transfers between devices: 68.4 us -> 7.16 us  [shifted(): return lax.ppermute(value, ('lsec', 'rsec'), pairs)]
    all_to_all x2 -> x0, waiting for transfers between devices: 41.3 us -> none  [from_everyone(): lax.all_to_all(jnp.broadcast_to(array[None], (size, *array.shape)), axis,...]
    ppermute x4 -> x2, waiting for transfers between devices: 139 us -> 106 us  [shifted(): return lax.ppermute(value, ('lsec', 'rsec'), pairs)]
    all_to_all x2 -> x0, starting transfers between devices: 17 us -> none  [from_everyone(): lax.all_to_all(jnp.broadcast_to(array[None], (size, *array.shape)), axis,...]
    dot_general x2, matrix products: 21.8 us -> 9.29 us  [the longest x1 4.81 us: on_device(): local = jnp.einsum('ab,rbc->rac', env_l, masked, precision=HI)]
    dot_general x1, matrix products: 12.8 us -> 7.3 us  [on_device(): source = jnp.einsum('ba,rbd->rad', oper_l, right_part, precision=HI)]
    dot_general x1, matrix products: 9.85 us -> 5.21 us  [on_device(): hop = jnp.einsum('ab,rbd->rad', oper_l, inner, precision=HI)]
  transfers between devices with their start and end apart: 8 -> 4, of which waited for: 6 -> 3; matrix products, arithmetic and copies ran while one was open for 19% -> 10% of each run, Pallas kernels for 0% -> 0%
where the time goes in v1:
time: 411 us
  waiting for transfers between devices  339 us (82%)
  matrix products  35.9 us (9%)
  between operations  14.8 us (4%)
  local copies, waits for them, and re-layouts  7.54 us (2%)
  starting transfers between devices  7.2 us (2%)
  other arithmetic  6.25 us (2%)
    all_gather x1, waiting for transfers between devices, on_device(): lax.all_gather(jnp.concatenate([right_env, right_op]), 'lsec', axis=1, ti...  150 us
    ppermute x2, waiting for transfers between devices, shifted(): return lax.ppermute(value, ('lsec', 'rsec'), pairs)  106 us
    all_gather x1, waiting for transfers between devices, on_device(): lax.all_gather(jnp.concatenate([left_env, left_op]), 'rsec', axis=1, tile...  83.2 us
  transfers between devices with their start and end apart: 4, of which 3 were waited for; matrix products, arithmetic and copies ran while one was open for 10% of the time, Pallas kernels for 0%

profile of v1, /device:TPU:198, one launch (start us, length us, event | category | flops | bytes accessed | tf_op | source)
XLA Modules:
  0.0 410.6 jit_solution(3178163259722050696)
XLA Ops:
  6.5 0.0 all-gather.5.cloned.1.call-start
  6.5 1.6 pad_maximum_fusion.1
  8.2 0.0 all-gather.5.cloned.1.call-update
  8.2 0.0 all-gather.3.cloned.1.call-start
  8.2 1.7 pad_maximum_fusion
  9.9 0.0 all-gather.3.cloned.1.call-update
  11.2 4.6 %copy.8 = f32[2,640,640]{1,2,0:T(8,128)} copy(f32[2,640,640]{2,1,0:T(8,128)} %param.7) | data formatting | bytes 6553600 | tf_op args[0]
  15.8 0.2 broadcast_multiply_fusion.1
  16.0 0.0 copy-start
  16.0 2.8 broadcast_multiply_fusion
  18.8 0.0 copy-done
  18.8 4.8 %collective-permute-start = (f32[2,640,640]{1,2,0:T(8,128)S(1)}, f32[2,640,640]{1,2,0:T(8,128)}, u32[]{:S(2)}, u32[]{:S(2)}) collective-permute-start(f32[2,640,640]{1,2,0:T(8,128)S(1)} %broadcast_multiply_fusion), channel_id=1, source_target_pairs={{1,16},{2,17},{3,18},{4,19},{5,20},{6,21},{7,22},{8,23},{9,24},{10... | collective-permute-start | bytes 9830408 | tf_op jit(solution)/shard_map/ppermute | solution.py:17
  23.6 150.1 %all-gather.5.cloned.1.call-done = f32[2,640,640]{2,1,0:T(8,128)} async-done(((f32[2,40,640]{2,1,0:T(8,128)}), f32[2,640,640]{2,1,0:T(8,128)}) %all-gather.5.cloned.1.call-update) | async-done | bytes 3276816 | tf_op jit(solution)/shard_map/all_gather | solution.py:29
  173.7 7.4 %fusion.4 = f32[2,640,640]{1,2,0:T(8,128)} fusion(f32[2,640,640]{1,2,0:T(8,128)S(1)} %broadcast_multiply_fusion, f32[2,640,640]{2,1,0:T(8,128)} %all-gather.5.cloned.1.call-done), kind=kOutput, calls=%fused_computation.12 | convolution fusion | flops 3145728000 | bytes 8192000 | tf_op jit(solution)/shard_map/rbc,cd->rbd/dot_general | solution.py:31
  181.1 83.2 %all-gather.3.cloned.1.call-done = f32[2,640,640]{2,1,0:T(8,128)} async-done(((f32[2,40,640]{2,1,0:T(8,128)}), f32[2,640,640]{2,1,0:T(8,128)}) %all-gather.3.cloned.1.call-update) | async-done | bytes 3276816 | tf_op jit(solution)/shard_map/all_gather | solution.py:28
  264.3 0.0 copy-start.3
  264.3 7.3 %convolution_bitcast_fusion = f32[2,640,640]{1,2,0:T(8,128)S(1)} fusion(f32[2,640,640]{1,2,0:T(8,128)} %fusion.4, f32[2,640,640]{2,1,0:T(8,128)} %all-gather.3.cloned.1.call-done), kind=kOutput, calls=%fused_computation.4 | convolution fusion | flops 3145728000 | bytes 8192000 | tf_op jit(solution)/shard_map/ba,rbd->rad/dot_general | solution.py:32
  271.6 0.0 copy-start.2
  271.6 2.4 collective-permute-start.1
  274.0 0.0 copy-done.3
  274.0 4.5 %fusion.2 = f32[2,640,640]{1,2,0:T(8,128)S(1)} fusion(f32[2,640,640]{1,2,0:T(8,128)S(1)} %broadcast_multiply_fusion, f32[2,640,640]{2,1,0:T(8,128)S(1)} %copy-done.3), kind=kOutput, calls=%fused_computation.8 | convolution fusion | flops 3145728000 | bytes 8192000 | tf_op jit(solution)/shard_map/rbc,dc->rbd/dot_general | solution.py:35
  278.5 0.0 copy-done.2
  278.5 4.8 %fusion.3 = f32[2,640,640]{2,1,0:T(8,128)S(1)} fusion(f32[2,640,640]{1,2,0:T(8,128)S(1)} %broadcast_multiply_fusion, f32[2,640,640]{2,1,0:T(8,128)S(1)} %copy-done.2), kind=kOutput, calls=%fused_computation.10 | convolution fusion | flops 3145728000 | bytes 8192000 | tf_op jit(solution)/shard_map/ab,rbc->rac/dot_general | solution.py:34
  283.3 0.0 copy-start.1
  283.3 0.0 collective-permute-done
  283.3 6.8 %fusion.5 = f32[2,640,640]{1,2,0:T(8,128)S(1)} fusion(f32[2,640,640]{1,2,0:T(8,128)} %collective-permute-done, f32[2,640,640]{2,1,0:T(8,128)S(1)} %copy-done.3), kind=kOutput, calls=%fused_computation.13 | convolution fusion | flops 3145728000 | bytes 8192000 | tf_op jit(solution)/shard_map/rbc,dc->rbd/dot_general | solution.py:36
  290.1 105.5 %collective-permute-done.1 = f32[2,640,640]{1,2,0:T(8,128)S(1)} collective-permute-done((f32[2,640,640]{1,2,0:T(8,128)S(1)}, f32[2,640,640]{1,2,0:T(8,128)S(1)}, u32[]{:S(2)}, u32[]{:S(2)}) %collective-permute-start.1) | collective-permute-done | bytes 3276832 | tf_op jit(solution)/shard_map/ppermute | solution.py:17
  395.6 0.0 copy-done.1
  395.6 5.2 %fusion.1 = f32[2,640,640]{1,2,0:T(8,128)S(1)} fusion(f32[2,640,640]{1,2,0:T(8,128)S(1)} %collective-permute-done.1, f32[2,640,640]{1,2,0:T(8,128)S(1)} %fusion.2, f32[2,640,640]{2,1,0:T(8,128)S(1)} %fusion.3, f32[2,640,640]{1,2,0:T(8,128)S(1)} %fusion.5, f32[640,640]{0,1:T(8,128)S(1)} %copy-done.1, f32[2,640,640]{2,1,0:T(8,128)S(1)} %copy-done.2), kind=kOutput, calls=%fused_computation.2 | convolution fusion | flops 3149004800 | bytes 19660800 | tf_op jit(solution)/shard_map/ab,rbd->rad/dot_general | solution.py:37
  400.8 3.0 copy.11
  (1 shorter events, 0.0 us)
Async XLA Ops:
  6.5 167.2 %all-gather.5.cloned.1.call-start = ((), (), s32[]{:S(2)}) async-start(), calls=%async_computation.1 | async-start | bytes 3481600 | tf_op jit(solution)/shard_map/all_gather | solution.py:29
  8.2 256.1 %all-gather.3.cloned.1.call-start = ((), (), s32[]{:S(2)}) async-start(), calls=%async_computation | async-start | bytes 3481600 | tf_op jit(solution)/shard_map/all_gather | solution.py:28
  16.0 2.8 copy-start
  18.8 264.5 %collective-permute-start = (f32[2,640,640]{1,2,0:T(8,128)S(1)}, f32[2,640,640]{1,2,0:T(8,128)}, u32[]{:S(2)}, u32[]{:S(2)}) collective-permute-start(f32[2,640,640]{1,2,0:T(8,128)S(1)} %broadcast_multiply_fusion), channel_id=1, source_target_pairs={{1,16},{2,17},{3,18},{4,19},{5,20},{6,21},{7,22},{8,23},{9,24},{10... | collective-permute-start | bytes 9830408 | tf_op jit(solution)/shard_map/ppermute | solution.py:17
  264.3 9.7 %copy-start.3 = (f32[2,640,640]{2,1,0:T(8,128)S(1)}, f32[2,640,640]{2,1,0:T(8,128)}, u32[]{:S(2)}) copy-start(f32[2,640,640]{2,1,0:T(8,128)} %all-gather.5.cloned.1.call-done) | copy-start | bytes 9830404
  271.6 6.9 %copy-start.2 = (f32[2,640,640]{2,1,0:T(8,128)S(1)}, f32[2,640,640]{2,1,0:T(8,128)}, u32[]{:S(2)}) copy-start(f32[2,640,640]{2,1,0:T(8,128)} %all-gather.3.cloned.1.call-done) | copy-start | bytes 9830404
  271.6 124.0 %collective-permute-start.1 = (f32[2,640,640]{1,2,0:T(8,128)S(1)}, f32[2,640,640]{1,2,0:T(8,128)S(1)}, u32[]{:S(2)}, u32[]{:S(2)}) collective-permute-start(f32[2,640,640]{1,2,0:T(8,128)S(1)} %convolution_bitcast_fusion), channel_id=1, source_target_pairs={{16,1},{17,2},{18,3},{19,4},{20,5},{21,6},{22,7},{23,8},{24,9},{25... | collective-permute-start | bytes 9830408 | tf_op jit(solution)/shard_map/ppermute | solution.py:17
  283.3 112.3 %copy-start.1 = (f32[640,640]{0,1:T(8,128)S(1)}, f32[640,640]{0,1:T(8,128)}, u32[]{:S(2)}) copy-start(f32[640,640]{0,1:T(8,128)} %copy-done) | copy-start | bytes 4915204
Sparse Core Ops, SparseCore 0:
  9.1 164.5 all-gather.4
  176.4 87.7 all-gather.2

commit v2 on v1

v2 whole, which is shorter than its diff:
```python
import jax
import jax.numpy as jnp
from jax import lax
from jax.experimental import pallas as pl
from jax.experimental.pallas import tpu as pltpu
from jax.sharding import PartitionSpec as P

MESH = pl.DeviceIdType.MESH
F32, BF16 = jnp.float32, jnp.bfloat16
W = 640
K = 8
C = 2 * W // K
FWD = 6
ENV, OP = 0, 1


def halves(value):
    high = value.astype(BF16)
    return high, (value - high.astype(F32)).astype(BF16)


def product(a, b, flip=False):
    dims = (((1,), (1 if flip else 0,)), ((), ()))

    def dot(u, v):
        return lax.dot_general(u, v, dims, preferred_element_type=F32)

    return dot(a[0], b[0]) + (dot(a[0], b[1]) + dot(a[1], b[0]))


def pick(cond, yes, no):
    return lax.select(cond, jnp.int32(yes), jnp.int32(no))


class Lane:
    def __init__(self, to, source, via, count, relay_from, relay_to, relay_count, last_leg):
        self.to, self.source = to, source
        self.via, self.count = via, count
        self.relay_from, self.relay_to, self.relay_count = relay_from, relay_to, relay_count
        self.last_leg = last_leg


def kernel(
    size_l, size_r, states, left_env, right_env, left_op, right_op, out,
    masked, masked_h, masked_l, hop, hop_relay, source, back, back_relay, lg, rg,
    lo_h, lo_l, lt_h, lt_l, le_h, le_l, ro_h, ro_l, re_h, re_l, mid_h, mid_l,
    hop_s, hop_r, hrel_s, hrel_r, back_s, back_r, brel_s, brel_r,
    lz_s, lz_r, ly_s, ly_r, lc_s, lc_r, rz_s, rz_r, rx_s, rx_r,
):
    i, j = lax.axis_index("lsec"), lax.axis_index("rsec")
    x, zl = lax.div(i, 4), lax.rem(i, 4)
    zh, y, c = lax.div(j, 8), lax.rem(lax.div(j, 2), 4), lax.rem(j, 2)
    up = ((i < 15) & (j > 0), i + 1, j - 1)
    down = ((i > 0) & (j < 15), i - 1, j + 1)

    h_wrap, h_cross = (zl == 3) & (c == 1) & (x < 3), (zl < 3) & (j == 8)
    h_rwrap, h_rcross = (zl == 3) & (c == 0) & (x > 0), (zl < 3) & (j == 15)
    h_lwrap, h_lcross = (zl == 0) & (c == 0) & (x > 0), (zl > 0) & (j == 7)
    lane_h = Lane(
        up, down,
        (pick(h_wrap, i + 4, i), pick(h_wrap, j - 1, 15)),
        pick(h_wrap, 2 * (x + 1), pick(h_cross, 4, 0)),
        (h_rwrap | h_rcross, pick(h_rwrap, i - 4, i), pick(h_rwrap, j + 1, 8)),
        (pick(h_rwrap, i - 3, i + 1), pick(h_rwrap, j, 7)),
        pick(h_rwrap, 2 * x, pick(h_rcross, 4, 0)),
        (h_lwrap | h_lcross, pick(h_lwrap, i + 3, i - 1), pick(h_lwrap, j, 15)),
    )
    b_wrap, b_cross = (zl == 0) & (c == 0) & (x > 0), (zl > 0) & (j == 7)
    b_rwrap, b_rcross = (zl == 0) & (c == 1) & (x < 3), (zl > 0) & (j == 0)
    b_lwrap, b_lcross = (zl == 3) & (c == 1) & (x < 3), (zl < 3) & (j == 8)
    lane_b = Lane(
        down, up,
        (pick(b_wrap, i - 4, i), pick(b_wrap, j + 1, 0)),
        pick(b_wrap, 2 * (4 - x), pick(b_cross, 4, 0)),
        (b_rwrap | b_rcross, pick(b_rwrap, i + 4, i), pick(b_rwrap, j - 1, 7)),
        (pick(b_rwrap, i + 3, i - 1), pick(b_rwrap, j, 8)),
        pick(b_rwrap, 2 * (3 - x), pick(b_rcross, 4, 0)),
        (b_lwrap | b_lcross, pick(b_lwrap, i - 3, i + 1), pick(b_lwrap, j, 0)),
    )

    other_zh = (i, lax.rem(j + 8, 16))
    other_core = (i, j + 1 - 2 * c)

    def along_y(step):
        return i, 8 * zh + 2 * lax.rem(y + step, 4) + c

    def along_z(step):
        return 4 * x + lax.rem(zl + step, 4), j

    def along_x(step):
        return lax.rem(i + 4 * step, 16), j

    bar = pltpu.get_barrier_semaphore()

    def greet(device):
        pl.semaphore_signal(bar, inc=1, device_id=device, device_id_type=MESH)

    greet(other_zh)
    greet(other_core)
    for step in (1, 2, 3):
        greet(along_y(step))
        greet(along_z(step))
        greet(along_x(step))
    expected = jnp.int32(11)
    for lane in (lane_h, lane_b):
        for ok, a, b in (lane.source, lane.relay_from, lane.last_leg):
            @pl.when(ok)
            def _():
                greet((a, b))
        expected = expected + pick(lane.to[0], 1, 0) + pick(lane.count > 0, 1, 0)
        expected = expected + pick(lane.relay_count > 0, 1, 0)
    pl.semaphore_wait(bar, expected)

    def remote(src, dst, send, recv, device):
        return pltpu.make_async_remote_copy(
            src_ref=src, dst_ref=dst, send_sem=send, recv_sem=recv,
            device_id=device, device_id_type=MESH,
        )

    left_in, right_in = (left_env, left_op), (right_env, right_op)

    def left_z(m):
        return remote(left_in[m].at[0], lg.at[m, zh, y, c], lz_s.at[m], lz_r.at[m], other_zh)

    def left_y(m, step):
        part = lg.at[m, :, y, c]
        return remote(part, part, ly_s.at[m, step - 1], ly_r.at[m, step - 1], along_y(step))

    def left_core(m):
        part = lg.at[m, :, :, c]
        return remote(part, part, lc_s.at[m], lc_r.at[m], other_core)

    def right_z(m, step):
        return remote(
            right_in[m].at[0], rg.at[m, x, zl], rz_s.at[m, step - 1], rz_r.at[m, step - 1], along_z(step)
        )

    def right_x(m, step):
        part = rg.at[m, x]
        return remote(part, part, rx_s.at[m, step - 1], rx_r.at[m, step - 1], along_x(step))

    steps = (1, 2, 3)
    for m in (OP, ENV):
        for step in steps:
            right_z(m, step).start()
        left_z(m).start()
    for m in (OP, ENV):
        lg[m, zh, y, c] = left_in[m][0]
        rg[m, x, zl] = right_in[m][0]

    def rows(k):
        return pl.ds(k * C, C)

    def straight(lane, k, src, dst, send, recv):
        return remote(src.at[rows(k)], dst.at[rows(k)], send.at[k], recv.at[k], lane.to[1:])

    def first_leg(lane, k, src, relay, send, recv):
        return remote(src.at[rows(k)], relay.at[rows(k)], send.at[k], recv.at[k], lane.via)

    def second_leg(lane, k, relay, dst, send, recv):
        return remote(relay.at[rows(k)], dst.at[rows(k)], send.at[k], recv.at[k], lane.relay_to)

    def ship(lane, k, src, dst, relay, send, recv, relay_recv):
        if k < FWD:
            @pl.when(k < lane.count)
            def _():
                first_leg(lane, k, src, relay, send, relay_recv).start()

        @pl.when(lane.to[0] & (k >= lane.count))
        def _():
            straight(lane, k, src, dst, send, recv).start()

    def ship_hop(k):
        ship(lane_h, k, masked, hop, hop_relay, hop_s, hop_r, hrel_r)

    def ship_back(k):
        ship(lane_b, k, source, back, back_relay, back_s, back_r, brel_r)

    def relay_hop(k):
        @pl.when(k < lane_h.relay_count)
        def _():
            first_leg(lane_h, k, masked, hop_relay, hop_s, hrel_r).wait_recv()
            second_leg(lane_h, k, hop_relay, hop, hrel_s, hop_r).start()

    def relay_back(k):
        @pl.when(k < lane_b.relay_count)
        def _():
            first_leg(lane_b, k, source, back_relay, back_s, brel_r).wait_recv()
            second_leg(lane_b, k, back_relay, back, brel_s, back_r).start()

    sl, sr = size_l[0], size_r[0]
    for k in range(K):
        row = lax.broadcasted_iota(jnp.int32, (C, W), 0) + (k % (K // 2)) * C
        col = lax.broadcasted_iota(jnp.int32, (C, W), 1)
        value = jnp.where((row < sl) & (col < sr), states[k * C : (k + 1) * C], 0.0)
        masked[k * C : (k + 1) * C] = value
        high, low = halves(value)
        masked_h[k * C : (k + 1) * C] = high
        masked_l[k * C : (k + 1) * C] = low
        ship_hop(k)

    @pl.when(jnp.logical_not(down[0]))
    def _():
        hop[...] = jnp.zeros_like(hop)

    @pl.when(jnp.logical_not(up[0]))
    def _():
        back[...] = jnp.zeros_like(back)

    for m in (OP, ENV):
        left_z(m).wait_recv()
        for step in steps:
            left_y(m, step).start()
        for step in steps:
            right_z(m, step).wait_recv()
        for step in steps:
            right_x(m, step).start()
    for m in (OP, ENV):
        for step in steps:
            left_y(m, step).wait_recv()
        left_core(m).start()
        relay_hop(m)

    def left_part(m, t):
        return lg[m, t // 4, t % 4].reshape(80, W)

    def right_part(m, t):
        return rg[m, t // 2, pl.ds((t % 2) * 2, 2)].reshape(80, W)

    def keep(part, m, into):
        for t in range(8):
            into[0][t * 80 : (t + 1) * 80], into[1][t * 80 : (t + 1) * 80] = halves(part(m, t))

    left_core(OP).wait_recv()
    keep(left_part, OP, (lo_h, lo_l))
    for t in range(W // 128):
        turned = lg[OP, :, :, :, :, t * 128 : (t + 1) * 128].reshape(W, 128).T
        lt_h[t * 128 : (t + 1) * 128], lt_l[t * 128 : (t + 1) * 128] = halves(turned)

    def pair(h, l, k, size):
        at = pl.ds(pl.multiple_of(k * size, size), size)
        return h[at, :], l[at, :]

    B = 320

    def left_times(l_h, l_l, m_h, m_l, k):
        return product(pair(l_h, l_l, k % 2, B), pair(m_h, m_l, k // 2, W))

    def put(k, value):
        at = pl.ds(pl.multiple_of(k * B, B), B)
        mid_h[at, :], mid_l[at, :] = halves(value)

    def at_left(k, _):
        put(k, left_times(lt_h, lt_l, masked_h, masked_l, k))
        return _

    lax.fori_loop(0, 4, at_left, 0)
    relay_hop(2)
    relay_hop(3)
    for step in steps:
        right_x(OP, step).wait_recv()
    keep(right_part, OP, (ro_h, ro_l))
    for k in range(K):
        source[rows(k), :] = product(
            (mid_h[rows(k), :], mid_l[rows(k), :]), (ro_h[...], ro_l[...])
        )
        ship_back(k)
        if k in (1, 3):
            relay_hop(4 + k // 2)

    left_core(ENV).wait_recv()
    keep(left_part, ENV, (le_h, le_l))
    for step in steps:
        right_x(ENV, step).wait_recv()
    keep(right_part, ENV, (re_h, re_l))

    def local(k, _):
        at = pl.ds(pl.multiple_of(k * B, B), B)
        out[at, :] = left_times(le_h, le_l, masked_h, masked_l, k) + product(
            pair(masked_h, masked_l, k, B), (re_h[...], re_l[...]), True
        )
        return _

    lax.fori_loop(0, 4, local, 0)
    for k in range(FWD):
        relay_back(k)

    def inner(k, _):
        at = pl.ds(pl.multiple_of(k * B, B), B)
        put(k, product(halves(hop[at, :]), (ro_h[...], ro_l[...]), True))
        return _

    def hopped(k, _):
        at = pl.ds(pl.multiple_of(k * B, B), B)
        out[at, :] += left_times(lo_h, lo_l, mid_h, mid_l, k)
        return _

    for root in range(2):
        for k in range(root * K // 2, (root + 1) * K // 2):
            @pl.when(down[0])
            def _():
                straight(lane_h, k, masked, hop, hop_s, hop_r).wait_recv()
        lax.fori_loop(2 * root, 2 * root + 2, inner, 0)
        lax.fori_loop(2 * root, 2 * root + 2, hopped, 0)

    for k in range(K):
        @pl.when(up[0])
        def _():
            straight(lane_b, k, source, back, back_s, back_r).wait_recv()

        out[rows(k), :] += back[rows(k), :]

    for m in (OP, ENV):
        left_z(m).wait_send()
        left_core(m).wait_send()
        for step in steps:
            left_y(m, step).wait_send()
            right_z(m, step).wait_send()
            right_x(m, step).wait_send()
    for k in range(K):
        @pl.when(up[0])
        def _():
            straight(lane_h, k, masked, hop, hop_s, hop_r).wait_send()

        @pl.when(down[0])
        def _():
            straight(lane_b, k, source, back, back_s, back_r).wait_send()
    for k in range(FWD):
        @pl.when(k < lane_h.relay_count)
        def _():
            second_leg(lane_h, k, hop_relay, hop, hrel_s, hop_r).wait_send()

        @pl.when(k < lane_b.relay_count)
        def _():
            second_leg(lane_b, k, back_relay, back, brel_s, back_r).wait_send()


def on_device(states, left_env, right_env, left_op, right_op, sizes_left, sizes_right):
    vmem = pl.BlockSpec(memory_space=pltpu.VMEM)
    smem = pl.BlockSpec(memory_space=pltpu.SMEM)
    whole, block = pltpu.VMEM((2 * W, W), F32), pltpu.VMEM((W, W), BF16)
    relay, half = pltpu.VMEM((FWD * C, W), F32), pltpu.VMEM((2 * W, W), BF16)
    dma = pltpu.SemaphoreType.DMA
    applied = pl.pallas_call(
        kernel,
        out_shape=jax.ShapeDtypeStruct((2 * W, W), F32),
        in_specs=[smem, smem] + [vmem] * 5,
        out_specs=vmem,
        scratch_shapes=[
            whole, half, half, whole, relay, whole, whole, relay,
            pltpu.VMEM((2, 2, 4, 2, 40, W), F32), pltpu.VMEM((2, 4, 4, 40, W), F32),
            *[block] * 10, half, half,
            dma((K,)), dma((K,)), dma((FWD,)), dma((FWD,)),
            dma((K,)), dma((K,)), dma((FWD,)), dma((FWD,)),
            dma((2,)), dma((2,)), dma((2, 3)), dma((2, 3)), dma((2,)), dma((2,)),
            dma((2, 3)), dma((2, 3)), dma((2, 3)), dma((2, 3)),
        ],
        compiler_params=pltpu.CompilerParams(
            collective_id=0, has_side_effects=True, vmem_limit_bytes=60 * 2**20
        ),
        cost_estimate=pl.CostEstimate(
            flops=24 * W**3, bytes_accessed=16 * W * W, transcendentals=0
        ),
    )(sizes_left, sizes_right, states.reshape(2 * W, W), left_env, right_env, left_op, right_op)
    places = jnp.arange(W, dtype=jnp.int32)
    mask = (places[:, None] < sizes_left[0]) & (places[None, :] < sizes_right[0])
    return jnp.where(mask[None], applied.reshape(2, W, W), 0.0)


def solution(mesh):
    in_specs = (
        P(None, "lsec", "rsec"),
        P("lsec", "rsec", None),
        P("rsec", "lsec", None),
        P("lsec", "rsec", None),
        P("rsec", "lsec", None),
        P("lsec"),
        P("rsec"),
    )
    out_specs = P(None, "lsec", "rsec")
    return jax.shard_map(
        on_device, mesh=mesh, in_specs=in_specs, out_specs=out_specs, check_vma=False
    )
```

time: 411 us -> 186 us (0.45)
  the two profiles are of different devices: /device:TPU:198 before, /device:TPU:164 now
where the time goes in v2:
time: 186 us
  Pallas kernels  181 us (97%)
  other arithmetic  4.2 us (2%)
    pallas_call x1, Pallas kernels, on_device(): pl.pallas_call(kernel, out_shape=jax.ShapeDtypeStruct((2 * W, W), F32), i...  181 us
    select_n x1, other arithmetic, on_device(): return jnp.where(mask[None], applied.reshape(2, W, W), 0.0)  3.94 us

profile of v2, /device:TPU:164, one launch (start us, length us, event | category | flops | bytes accessed | tf_op | source)
XLA Modules:
  0.0 186.2 jit_solution(958780856439442177)
XLA Ops:
  1.3 0.3 broadcast_and_fusion
  1.6 180.7 %shard_map.73 = f32[1280,640]{1,0:T(8,128)} custom-call(s32[1]{0:T(128)} %copy.8.size_l, s32[1]{0:T(128)} %copy.9.size_r, f32[1280,640]{1,0:T(8,128)} %bitcast.7, f32[1,40,640]{2,1,0:T(8,128)} %left_env.1, f32[1,40,640]{2,1,0:T(8,128)} %right_env.1, f32[1,40,640]{2,1,0:T(8,128)} %left_op.1, f32[1,40,640]{2,1,0:T(8,128)} %right_op.1), custom_call_target="tpu_custom_call" | custom-call | flops 6291456000 | bytes 6553600 | tf_op jit(solution)/shard_map/pallas_call | solution.py:344
  182.3 3.9 %broadcast_select_fusion = f32[2,640,640]{2,1,0:T(8,128)} fusion(f32[2,640,640]{2,1,0:T(8,128)} %bitcast.6, pred[640,640]{1,0:T(8,128)(4,1)S(1)} %broadcast_and_fusion), kind=kLoop, calls=%fused_computation | loop fusion | flops 819200 | bytes 6963200 | tf_op jit(solution)/shard_map/jit(_where)/select_n | solution.py:367
  (1 shorter events, 0.0 us)

commit v3 on v2

--- a/solution.py
+++ b/solution.py
@@ -32,12 +32,48 @@
     return lax.select(cond, jnp.int32(yes), jnp.int32(no))
 
 
+INSIDE = {(0, 0): 1, (0, 1): 6, (0, 2): 4, (1, 1): 1, (1, 2): 2, (3, 0): 2, (3, 1): 1}
+EDGE = {
+    (0, 0, 1, 1): 3, (0, 0, 2, 1): 1, (0, 1, 0, 1): 1, (0, 1, 1, 0): 1, (0, 1, 1, 1): 2, (0, 1, 2, 0): 1,
+    (0, 1, 2, 1): 2, (0, 1, 3, 0): 1, (0, 1, 3, 1): 4, (1, 0, 1, 1): 6, (1, 0, 2, 1): 2, (1, 1, 0, 1): 3,
+    (1, 1, 1, 1): 6, (1, 1, 2, 1): 6, (1, 1, 3, 0): 3, (1, 1, 3, 1): 6, (2, 0, 1, 0): 3, (2, 0, 1, 1): 6,
+    (2, 0, 2, 0): 3, (2, 1, 0, 1): 4, (2, 1, 1, 0): 3, (2, 1, 1, 1): 6, (2, 1, 2, 0): 6, (2, 1, 2, 1): 6,
+    (2, 1, 3, 0): 6, (2, 1, 3, 1): 5,
+}
+
+
+def detours(x, zl, j):
+    total = jnp.int32(0)
+    edge = 16 * x + j
+    inside = 4 * j + zl
+    for (px, pz, py, pc), n in EDGE.items():
+        total = pick((zl == 3) & (edge == 16 * px + 8 * pz + 2 * py + pc), n, total)
+    for (py, pl_), n in INSIDE.items():
+        total = pick(inside == 4 * (8 + 2 * py) + pl_, n, total)
+    return total
+
+
 class Lane:
-    def __init__(self, to, source, via, count, relay_from, relay_to, relay_count, last_leg):
-        self.to, self.source = to, source
-        self.via, self.count = via, count
-        self.relay_from, self.relay_to, self.relay_count = relay_from, relay_to, relay_count
-        self.last_leg = last_leg
+    def __init__(self, i, j, mirrored):
+        def place(p, q):
+            return (15 - p, 15 - q) if mirrored else (p, q)
+
+        def by_way_of(p, q):
+            return 4 * lax.div(p + 1, 4) + lax.rem(p, 4), 8 * lax.div(q, 8) + lax.rem(q + 7, 8)
+
+        p, q = place(i, j)
+        x, zl = lax.div(p, 4), lax.rem(p, 4)
+        self.to_ok, self.to = (p < 15) & (q > 0), place(p + 1, q - 1)
+        self.from_ok, self.source = (p > 0) & (q < 15), place(p - 1, q + 1)
+        self.via = place(*by_way_of(p, q))
+        self.count = pick(self.to_ok, detours(x, zl, q), 0)
+        back_x = pick(zl == 3, x - 1, x)
+        sp, sq = 4 * back_x + zl, 8 * lax.div(q, 8) + lax.rem(q + 1, 8)
+        self.relay_from, self.relay_to = place(sp, sq), place(sp + 1, sq - 1)
+        self.relay_count = pick((sp >= 0) & (sp < 15) & (sq > 0), detours(back_x, zl, sq), 0)
+        lp, lq = lax.rem(p + 15, 16), lax.rem(q + 1, 16)
+        self.last_leg = place(*by_way_of(lp, lq))
+        self.last_count = pick(self.from_ok, detours(lax.div(lp, 4), lax.rem(lp, 4), lq), 0)
 
 
 def kernel(
@@ -50,33 +86,7 @@
     i, j = lax.axis_index("lsec"), lax.axis_index("rsec")
     x, zl = lax.div(i, 4), lax.rem(i, 4)
     zh, y, c = lax.div(j, 8), lax.rem(lax.div(j, 2), 4), lax.rem(j, 2)
-    up = ((i < 15) & (j > 0), i + 1, j - 1)
-    down = ((i > 0) & (j < 15), i - 1, j + 1)
-
-    h_wrap, h_cross = (zl == 3) & (c == 1) & (x < 3), (zl < 3) & (j == 8)
-    h_rwrap, h_rcross = (zl == 3) & (c == 0) & (x > 0), (zl < 3) & (j == 15)
-    h_lwrap, h_lcross = (zl == 0) & (c == 0) & (x > 0), (zl > 0) & (j == 7)
-    lane_h = Lane(
-        up, down,
-        (pick(h_wrap, i + 4, i), pick(h_wrap, j - 1, 15)),
-        pick(h_wrap, 2 * (x + 1), pick(h_cross, 4, 0)),
-        (h_rwrap | h_rcross, pick(h_rwrap, i - 4, i), pick(h_rwrap, j + 1, 8)),
-        (pick(h_rwrap, i - 3, i + 1), pick(h_rwrap, j, 7)),
-        pick(h_rwrap, 2 * x, pick(h_rcross, 4, 0)),
-        (h_lwrap | h_lcross, pick(h_lwrap, i + 3, i - 1), pick(h_lwrap, j, 15)),
-    )
-    b_wrap, b_cross = (zl == 0) & (c == 0) & (x > 0), (zl > 0) & (j == 7)
-    b_rwrap, b_rcross = (zl == 0) & (c == 1) & (x < 3), (zl > 0) & (j == 0)
-    b_lwrap, b_lcross = (zl == 3) & (c == 1) & (x < 3), (zl < 3) & (j == 8)
-    lane_b = Lane(
-        down, up,
-        (pick(b_wrap, i - 4, i), pick(b_wrap, j + 1, 0)),
-        pick(b_wrap, 2 * (4 - x), pick(b_cross, 4, 0)),
-        (b_rwrap | b_rcross, pick(b_rwrap, i + 4, i), pick(b_rwrap, j - 1, 7)),
-        (pick(b_rwrap, i + 3, i - 1), pick(b_rwrap, j, 8)),
-        pick(b_rwrap, 2 * (3 - x), pick(b_rcross, 4, 0)),
-        (b_lwrap | b_lcross, pick(b_lwrap, i - 3, i + 1), pick(b_lwrap, j, 0)),
-    )
+    lane_h, lane_b = Lane(i, j, False), Lane(i, j, True)
 
     other_zh = (i, lax.rem(j + 8, 16))
     other_core = (i, j + 1 - 2 * c)
@@ -84,8 +94,7 @@
     def along_y(step):
         return i, 8 * zh + 2 * lax.rem(y + step, 4) + c
 
-    def along_z(step):
-        return 4 * x + lax.rem(zl + step, 4), j
+    z_next = ((zl < 3, i + 1), (zl > 0, i - 1))
 
     def along_x(step):
         return lax.rem(i + 4 * step, 16), j
@@ -99,15 +108,25 @@
     greet(other_core)
     for step in (1, 2, 3):
         greet(along_y(step))
-        greet(along_z(step))
         greet(along_x(step))
-    expected = jnp.int32(11)
+    expected = jnp.int32(8)
+    for ok, a in z_next:
+        @pl.when(ok)
+        def _():
+            greet((a, j))
+
+        expected = expected + pick(ok, 1, 0)
     for lane in (lane_h, lane_b):
-        for ok, a, b in (lane.source, lane.relay_from, lane.last_leg):
+        for ok, device in (
+            (lane.from_ok, lane.source),
+            (lane.relay_count > 0, lane.relay_from),
+            (lane.last_count > 0, lane.last_leg),
+        ):
             @pl.when(ok)
             def _():
-                greet((a, b))
-        expected = expected + pick(lane.to[0], 1, 0) + pick(lane.count > 0, 1, 0)
+                greet(device)
+
+        expected = expected + pick(lane.to_ok, 1, 0) + pick(lane.count > 0, 1, 0)
         expected = expected + pick(lane.relay_count > 0, 1, 0)
     pl.semaphore_wait(bar, expected)
 
@@ -130,20 +149,39 @@
         part = lg.at[m, :, :, c]
         return remote(part, part, lc_s.at[m], lc_r.at[m], other_core)
 
-    def right_z(m, step):
-        return remote(
-            right_in[m].at[0], rg.at[m, x, zl], rz_s.at[m, step - 1], rz_r.at[m, step - 1], along_z(step)
+    def right_z(m, step, way, arriving=False):
+        back = step if arriving else step - 1
+        owner = zl - back if way == 0 else zl + back
+        part = rg.at[m, x, owner]
+        src = right_in[m].at[0] if step == 1 and not arriving else part
+        copy = remote(
+            src, part, rz_s.at[m, way, step - 1], rz_r.at[m, way, step - 1], (z_next[way][1], j)
         )
+        return (z_next[way][0] | arriving) & (owner >= 0) & (owner <= 3), copy
+
+    def right_z_start(m, step):
+        for way in (0, 1):
+            ok, copy = right_z(m, step, way)
+
+            @pl.when(ok)
+            def _():
+                copy.start()
+
+    def right_z_arrive(m, step):
+        for way in (0, 1):
+            ok, copy = right_z(m, step, way, True)
+
+            @pl.when(ok)
+            def _():
+                copy.wait_recv()
 
     def right_x(m, step):
         part = rg.at[m, x]
         return remote(part, part, rx_s.at[m, step - 1], rx_r.at[m, step - 1], along_x(step))
 
     steps = (1, 2, 3)
-    for m in (OP, ENV):
-        for step in steps:
-            right_z(m, step).start()
-        left_z(m).start()
+    right_z_start(OP, 1)
+    left_z(OP).start()
     for m in (OP, ENV):
         lg[m, zh, y, c] = left_in[m][0]
         rg[m, x, zl] = right_in[m][0]
@@ -152,7 +190,7 @@
         return pl.ds(k * C, C)
 
     def straight(lane, k, src, dst, send, recv):
-        return remote(src.at[rows(k)], dst.at[rows(k)], send.at[k], recv.at[k], lane.to[1:])
+        return remote(src.at[rows(k)], dst.at[rows(k)], send.at[k], recv.at[k], lane.to)
 
     def first_leg(lane, k, src, relay, send, recv):
         return remote(src.at[rows(k)], relay.at[rows(k)], send.at[k], recv.at[k], lane.via)
@@ -166,7 +204,7 @@
             def _():
                 first_leg(lane, k, src, relay, send, relay_recv).start()
 
-        @pl.when(lane.to[0] & (k >= lane.count))
+        @pl.when(lane.to_ok & (k >= lane.count))
         def _():
             straight(lane, k, src, dst, send, recv).start()
 
@@ -197,29 +235,55 @@
         high, low = halves(value)
         masked_h[k * C : (k + 1) * C] = high
         masked_l[k * C : (k + 1) * C] = low
-        ship_hop(k)
-
-    @pl.when(jnp.logical_not(down[0]))
+        if k < 2:
+            ship_hop(k)
+
+    @pl.when(jnp.logical_not(lane_h.from_ok))
     def _():
         hop[...] = jnp.zeros_like(hop)
 
-    @pl.when(jnp.logical_not(up[0]))
+    @pl.when(jnp.logical_not(lane_b.from_ok))
     def _():
         back[...] = jnp.zeros_like(back)
 
-    for m in (OP, ENV):
+    def left_y_start(m):
         left_z(m).wait_recv()
         for step in steps:
             left_y(m, step).start()
-        for step in steps:
-            right_z(m, step).wait_recv()
+
+    def right_x_start(m):
+        right_z_arrive(m, 3)
         for step in steps:
             right_x(m, step).start()
-    for m in (OP, ENV):
-        for step in steps:
-            left_y(m, step).wait_recv()
-        left_core(m).start()
-        relay_hop(m)
+
+    right_z_arrive(OP, 1)
+    right_z_start(OP, 2)
+    left_z(ENV).start()
+    ship_hop(2)
+    left_y_start(OP)
+    right_z_arrive(OP, 2)
+    right_z_start(OP, 3)
+    right_z_start(ENV, 1)
+    ship_hop(3)
+    right_x_start(OP)
+    ship_hop(4)
+    right_z_arrive(ENV, 1)
+    right_z_start(ENV, 2)
+    left_y_start(ENV)
+    ship_hop(5)
+    relay_hop(0)
+    right_z_arrive(ENV, 2)
+    right_z_start(ENV, 3)
+    ship_hop(6)
+    ship_hop(7)
+    for step in steps:
+        left_y(OP, step).wait_recv()
+    left_core(OP).start()
+    right_x_start(ENV)
+    relay_hop(1)
+    for step in steps:
+        left_y(ENV, step).wait_recv()
+    left_core(ENV).start()
 
     def left_part(m, t):
         return lg[m, t // 4, t % 4].reshape(80, W)
@@ -285,26 +349,24 @@
     for k in range(FWD):
         relay_back(k)
 
-    def inner(k, _):
-        at = pl.ds(pl.multiple_of(k * B, B), B)
-        put(k, product(halves(hop[at, :]), (ro_h[...], ro_l[...]), True))
-        return _
-
     def hopped(k, _):
         at = pl.ds(pl.multiple_of(k * B, B), B)
         out[at, :] += left_times(lo_h, lo_l, mid_h, mid_l, k)
         return _
 
-    for root in range(2):
-        for k in range(root * K // 2, (root + 1) * K // 2):
-            @pl.when(down[0])
-            def _():
-                straight(lane_h, k, masked, hop, hop_s, hop_r).wait_recv()
-        lax.fori_loop(2 * root, 2 * root + 2, inner, 0)
-        lax.fori_loop(2 * root, 2 * root + 2, hopped, 0)
-
     for k in range(K):
-        @pl.when(up[0])
+        @pl.when(lane_h.from_ok)
+        def _():
+            straight(lane_h, k, masked, hop, hop_s, hop_r).wait_recv()
+
+        mid_h[rows(k), :], mid_l[rows(k), :] = halves(
+            product(halves(hop[rows(k), :]), (ro_h[...], ro_l[...]), True)
+        )
+        if k % (K // 2) == K // 2 - 1:
+            lax.fori_loop(k // 2 - 1, k // 2 + 1, hopped, 0)
+
+    for k in range(K):
+        @pl.when(lane_b.from_ok)
         def _():
             straight(lane_b, k, source, back, back_s, back_r).wait_recv()
 
@@ -315,14 +377,19 @@
         left_core(m).wait_send()
         for step in steps:
             left_y(m, step).wait_send()
-            right_z(m, step).wait_send()
             right_x(m, step).wait_send()
+            for way in (0, 1):
+                ok, copy = right_z(m, step, way)
+
+                @pl.when(ok)
+                def _():
+                    copy.wait_send()
     for k in range(K):
-        @pl.when(up[0])
+        @pl.when(lane_h.to_ok)
         def _():
             straight(lane_h, k, masked, hop, hop_s, hop_r).wait_send()
 
-        @pl.when(down[0])
+        @pl.when(lane_b.to_ok)
         def _():
             straight(lane_b, k, source, back, back_s, back_r).wait_send()
     for k in range(FWD):
@@ -353,10 +420,10 @@
             dma((K,)), dma((K,)), dma((FWD,)), dma((FWD,)),
             dma((K,)), dma((K,)), dma((FWD,)), dma((FWD,)),
             dma((2,)), dma((2,)), dma((2, 3)), dma((2, 3)), dma((2,)), dma((2,)),
-            dma((2, 3)), dma((2, 3)), dma((2, 3)), dma((2, 3)),
+            dma((2, 2, 3)), dma((2, 2, 3)), dma((2, 3)), dma((2, 3)),
         ],
         compiler_params=pltpu.CompilerParams(
-            collective_id=0, has_side_effects=True, vmem_limit_bytes=60 * 2**20
+            collective_id=0, has_side_effects=True, vmem_limit_bytes=48 * 2**20
         ),
         cost_estimate=pl.CostEstimate(
             flops=24 * W**3, bytes_accessed=16 * W * W, transcendentals=0

time: 186 us -> 208 us (1.12)
  the two profiles are of different devices: /device:TPU:164 before, /device:TPU:225 now
where the time goes in v3:
time: 208 us; the launch traced here: 207 us
  Pallas kernels  200 us (96%)
  local copies, waits for them, and re-layouts  3.57 us (2%)
  other arithmetic  2.28 us (1%)
    pallas_call x1, Pallas kernels, on_device(): pl.pallas_call(kernel, out_shape=jax.ShapeDtypeStruct((2 * W, W), F32), i...  200 us

profile of v3, /device:TPU:225, one launch (start us, length us, event | category | flops | bytes accessed | tf_op | source)
XLA Modules:
  0.0 207.4 jit_solution(6616847183586825500)
XLA Ops:
  1.3 0.3 broadcast_and_fusion
  1.6 0.0 copy-start
  1.6 0.9 copy-done
  2.5 0.0 copy-start.1
  2.5 0.9 copy-done.1
  3.4 0.0 copy-start.2
  3.4 0.9 copy-done.2
  4.3 0.0 copy-start.3
  4.3 0.9 copy-done.3
  5.2 200.2 %shard_map.73 = f32[1280,640]{1,0:T(8,128)S(1)} custom-call(s32[1]{0:T(128)} %copy.8.size_l, s32[1]{0:T(128)} %copy.9.size_r, f32[1280,640]{1,0:T(8,128)} %bitcast.7, f32[1,40,640]{2,1,0:T(8,128)S(1)} %copy-done, f32[1,40,640]{2,1,0:T(8,128)S(1)} %copy-done.1, f32[1,40,640]{2,1,0:T(8,128)S(1)} %copy-done.2, f32[1,40,640]{2,1,0:T(8,128)S(1)} %copy-done.3), custom_call_target="tpu_custom_call" | custom-call | flops 6291456000 | bytes 6553600 | tf_op jit(solution)/shard_map/pallas_call | solution.py:411
  205.4 2.0 broadcast_select_fusion
  (1 shorter events, 0.0 us)
Async XLA Ops:
  1.6 0.9 copy-start
  2.5 0.9 copy-start.1
  3.4 0.9 copy-start.2
  4.3 0.9 copy-start.3

commit v4 on v2

--- a/solution.py
+++ b/solution.py
@@ -160,21 +160,20 @@
     def second_leg(lane, k, relay, dst, send, recv):
         return remote(relay.at[rows(k)], dst.at[rows(k)], send.at[k], recv.at[k], lane.relay_to)
 
-    def ship(lane, k, src, dst, relay, send, recv, relay_recv):
+    def ship_straight(lane, k, src, dst, send, recv):
+        @pl.when(lane.to[0] & (k >= lane.count))
+        def _():
+            straight(lane, k, src, dst, send, recv).start()
+
+    def ship_first_leg(lane, k, src, relay, send, relay_recv):
+        @pl.when(k < lane.count)
+        def _():
+            first_leg(lane, k, src, relay, send, relay_recv).start()
+
+    def ship_back(k):
         if k < FWD:
-            @pl.when(k < lane.count)
-            def _():
-                first_leg(lane, k, src, relay, send, relay_recv).start()
-
-        @pl.when(lane.to[0] & (k >= lane.count))
-        def _():
-            straight(lane, k, src, dst, send, recv).start()
-
-    def ship_hop(k):
-        ship(lane_h, k, masked, hop, hop_relay, hop_s, hop_r, hrel_r)
-
-    def ship_back(k):
-        ship(lane_b, k, source, back, back_relay, back_s, back_r, brel_r)
+            ship_first_leg(lane_b, k, source, back_relay, back_s, brel_r)
+        ship_straight(lane_b, k, source, back, back_s, back_r)
 
     def relay_hop(k):
         @pl.when(k < lane_h.relay_count)
@@ -197,7 +196,7 @@
         high, low = halves(value)
         masked_h[k * C : (k + 1) * C] = high
         masked_l[k * C : (k + 1) * C] = low
-        ship_hop(k)
+        ship_straight(lane_h, k, masked, hop, hop_s, hop_r)
 
     @pl.when(jnp.logical_not(down[0]))
     def _():
@@ -215,11 +214,13 @@
             right_z(m, step).wait_recv()
         for step in steps:
             right_x(m, step).start()
+        if m == OP:
+            for k in range(FWD):
+                ship_first_leg(lane_h, k, masked, hop_relay, hop_s, hrel_r)
     for m in (OP, ENV):
         for step in steps:
             left_y(m, step).wait_recv()
         left_core(m).start()
-        relay_hop(m)
 
     def left_part(m, t):
         return lg[m, t // 4, t % 4].reshape(80, W)
@@ -255,8 +256,8 @@
         return _
 
     lax.fori_loop(0, 4, at_left, 0)
-    relay_hop(2)
-    relay_hop(3)
+    relay_hop(0)
+    relay_hop(1)
     for step in steps:
         right_x(OP, step).wait_recv()
     keep(right_part, OP, (ro_h, ro_l))
@@ -265,8 +266,8 @@
             (mid_h[rows(k), :], mid_l[rows(k), :]), (ro_h[...], ro_l[...])
         )
         ship_back(k)
-        if k in (1, 3):
-            relay_hop(4 + k // 2)
+        if 2 <= k < FWD:
+            relay_hop(k)
 
     left_core(ENV).wait_recv()
     keep(left_part, ENV, (le_h, le_l))
@@ -281,27 +282,25 @@
         )
         return _
 
-    lax.fori_loop(0, 4, local, 0)
     for k in range(FWD):
         relay_back(k)
-
-    def inner(k, _):
-        at = pl.ds(pl.multiple_of(k * B, B), B)
-        put(k, product(halves(hop[at, :]), (ro_h[...], ro_l[...]), True))
-        return _
+    lax.fori_loop(0, 4, local, 0)
 
     def hopped(k, _):
         at = pl.ds(pl.multiple_of(k * B, B), B)
         out[at, :] += left_times(lo_h, lo_l, mid_h, mid_l, k)
         return _
 
-    for root in range(2):
-        for k in range(root * K // 2, (root + 1) * K // 2):
-            @pl.when(down[0])
-            def _():
-                straight(lane_h, k, masked, hop, hop_s, hop_r).wait_recv()
-        lax.fori_loop(2 * root, 2 * root + 2, inner, 0)
-        lax.fori_loop(2 * root, 2 * root + 2, hopped, 0)
+    for k in range(K):
+        @pl.when(down[0])
+        def _():
+            straight(lane_h, k, masked, hop, hop_s, hop_r).wait_recv()
+
+        mid_h[rows(k), :], mid_l[rows(k), :] = halves(
+            product(halves(hop[rows(k), :]), (ro_h[...], ro_l[...]), True)
+        )
+        if k % (K // 2) == K // 2 - 1:
+            lax.fori_loop(k // 2 - 1, k // 2 + 1, hopped, 0)
 
     for k in range(K):
         @pl.when(up[0])
@@ -356,7 +355,7 @@
             dma((2, 3)), dma((2, 3)), dma((2, 3)), dma((2, 3)),
         ],
         compiler_params=pltpu.CompilerParams(
-            collective_id=0, has_side_effects=True, vmem_limit_bytes=60 * 2**20
+            collective_id=0, has_side_effects=True, vmem_limit_bytes=48 * 2**20
         ),
         cost_estimate=pl.CostEstimate(
             flops=24 * W**3, bytes_accessed=16 * W * W, transcendentals=0

time: 186 us -> 183 us (0.984)
  the two profiles are of different devices: /device:TPU:164 before, /device:TPU:21 now
where the time goes in v4:
time: 183 us
  Pallas kernels  176 us (96%)
  local copies, waits for them, and re-layouts  3.57 us (2%)
  other arithmetic  2.28 us (1%)
    pallas_call x1, Pallas kernels, on_device(): pl.pallas_call(kernel, out_shape=jax.ShapeDtypeStruct((2 * W, W), F32), i...  176 us

profile of v4, /device:TPU:21, one launch (start us, length us, event | category | flops | bytes accessed | tf_op | source)
XLA Modules:
  0.0 183.0 jit_solution(208636935272886929)
XLA Ops:
  1.3 0.3 broadcast_and_fusion
  1.6 0.0 copy-start
  1.6 0.9 copy-done
  2.5 0.0 copy-start.1
  2.5 0.9 copy-done.1
  3.4 0.0 copy-start.2
  3.4 0.9 copy-done.2
  4.3 0.0 copy-start.3
  4.3 0.9 copy-done.3
  5.2 175.8 %shard_map.73 = f32[1280,640]{1,0:T(8,128)S(1)} custom-call(s32[1]{0:T(128)} %copy.8.size_l, s32[1]{0:T(128)} %copy.9.size_r, f32[1280,640]{1,0:T(8,128)} %bitcast.7, f32[1,40,640]{2,1,0:T(8,128)S(1)} %copy-done, f32[1,40,640]{2,1,0:T(8,128)S(1)} %copy-done.1, f32[1,40,640]{2,1,0:T(8,128)S(1)} %copy-done.2, f32[1,40,640]{2,1,0:T(8,128)S(1)} %copy-done.3), custom_call_target="tpu_custom_call" | custom-call | flops 6291456000 | bytes 6553600 | tf_op jit(solution)/shard_map/pallas_call | solution.py:343
  181.0 2.0 %broadcast_select_fusion = f32[2,640,640]{2,1,0:T(8,128)} fusion(f32[2,640,640]{2,1,0:T(8,128)S(1)} %bitcast.6, pred[640,640]{1,0:T(8,128)(4,1)S(1)} %broadcast_and_fusion), kind=kLoop, calls=%fused_computation | loop fusion | flops 819200 | bytes 6963200 | tf_op jit(solution)/shard_map/jit(_where)/select_n | solution.py:366
  (1 shorter events, 0.0 us)
Async XLA Ops:
  1.6 0.9 copy-start
  2.5 0.9 copy-start.1
  3.4 0.9 copy-start.2
  4.3 0.9 copy-start.3
